TPU v7x, 32 devices: a whole 2x2x4 slice. The times are simulated.
32 devices in a mesh: groups: 2 (over x), tensor: 8 (over z, y), role: 2 (over core).
Axes of the slice: x: 2, y: 2, z: 4, core: 2. Of those that a mesh axis runs over, the one named last changes fastest.
Arguments:
- stream_in: bfloat16 [256, 8192], P(('groups', 'tensor', 'role')), parts along dimension 0, may hold values from -6 to 6
- norm_gain: bfloat16 [8192], replicated, may hold values from 0.099609375 to 1.8984375
- w_query: bfloat16 [8192, 2048], P(None, ('tensor', 'role')), may hold values from -0.0625 to 0.0625
- w_keyval: bfloat16 [8192, 512], P(None, ('tensor', 'role')), may hold values from -0.0625 to 0.0625
- w_out: bfloat16 [2048, 8192], P(('tensor', 'role')), may hold values from -0.125 to 0.125
- prefix_cache: bfloat16 [8192, 512], P(('groups', 'tensor', 'role')), parts along dimension 0, as said below
- span_lens: int32 [16], P('groups'), parts along dimension 0, may hold values from 1 to 64, 128 in all
- prefix_lens: int32 [16], P('groups'), parts along dimension 0, may hold values from 1 to 2048, 4096 in all
- owner_dev: int32 [16], P('groups'), parts along dimension 0, may hold values from 0 to 15, as said below
- offsets: int32 [16], P('groups'), parts along dimension 0, may hold values from 0 to 384
- decode_cache: bfloat16 [16384, 512], P(('groups', 'tensor', 'role')), parts along dimension 0, may hold values from -6 to 6
Outputs:
- stream_out: bfloat16 [256, 8192], P(('groups', 'tensor', 'role')), parts along dimension 0
- cache_out: bfloat16 [16384, 512], P(('groups', 'tensor', 'role')), parts along dimension 0
There are 2 independent parts, one for each index of `groups`. A program takes and returns all parts, laid end to end along the dimension named above; an argument that names none is the same for every part. Nothing has to cross between parts.
Inputs may be any that keep to these rules, and one draw needn't show every extreme that they name: `owner_dev`: the owners are distinct device indices. `prefix_cache`: a few prefix keys may be of large magnitude.
All inputs are finite; a program needn't handle non-finite values.
Results may differ from a plain program's by a relative error of at most 0.012.
The roundings to bfloat16 on the way count: a program that leaves them out, or rounds other values in their place, can miss the bound.
Values may be sent and summed in bfloat16 or wider, within the bound.
A program may use at most 128 MiB of HBM per device.

v0:
```python
import jax
import jax.numpy as jnp
from jax import lax
from jax.sharding import PartitionSpec as P

HEAD = 128
GROUP = 8


epsilon = 1e-05
negative = -1e30


def segment_of(positions, lengths):
    run_ends = jnp.cumsum(lengths)
    return jnp.sum((positions[:, None] >= run_ends[None, :]).astype(jnp.int32), axis=1)


def shards(
    stream_in,
    norm_gain,
    w_query,
    w_keyval,
    w_out,
    prefix_cache,
    span_lens,
    prefix_lens,
    owner_dev,
    offsets,
    decode_cache,
):
    devices = lax.axis_size(("tensor", "role"))
    myself = lax.axis_index(("tensor", "role"))
    span_rows = stream_in.shape[0] * devices
    local_pre = prefix_cache.shape[0]
    kv_heads = devices // GROUP
    score_scale = 1.0 / HEAD**0.5
    floats = stream_in.astype(jnp.float32)
    normed = (
        floats
        * lax.rsqrt(jnp.mean(floats * floats, axis=1, keepdims=True) + epsilon)
        * norm_gain.astype(jnp.float32)
    ).astype(jnp.bfloat16)
    shard_rows = lax.all_gather(normed, ("tensor", "role"), axis=0, tiled=True)
    projected = jnp.concatenate(
        [
            jnp.dot(shard_rows, w_query, preferred_element_type=jnp.float32),
            jnp.dot(shard_rows, w_keyval, preferred_element_type=jnp.float32),
        ],
        axis=1,
    )
    queries = projected[:, :HEAD].astype(jnp.bfloat16)
    kv_local = projected[:, HEAD:].astype(jnp.bfloat16)
    keyval = lax.all_gather(kv_local, ("tensor", "role"), axis=1, tiled=True)
    column_base = myself // GROUP * (2 * HEAD)
    span_keys = lax.dynamic_slice_in_dim(keyval, column_base, HEAD, 1)
    span_values = lax.dynamic_slice_in_dim(keyval, column_base + HEAD, HEAD, 1)
    row_index = jnp.arange(span_rows, dtype=jnp.int32)
    tok_seg = segment_of(row_index, span_lens)
    span_mask = (tok_seg[:, None] == tok_seg[None, :]) & (row_index[:, None] >= row_index[None, :])
    span_scores = jnp.where(
        span_mask,
        jnp.dot(queries, span_keys.T, preferred_element_type=jnp.float32) * score_scale,
        negative,
    )
    stored = jnp.transpose(prefix_cache.reshape(local_pre, kv_heads, 2 * HEAD), (1, 0, 2))
    span_max = jnp.max(span_scores, axis=1)
    span_weights = jnp.where(span_mask, jnp.exp(span_scores - span_max[:, None]), 0.0)
    start_carry = (
        span_max,
        jnp.sum(span_weights, axis=1),
        jnp.dot(span_weights.astype(jnp.bfloat16), span_values, preferred_element_type=jnp.float32),
    )
    repeated = jnp.repeat(stored, GROUP, axis=0)
    received = lax.all_to_all(repeated, ("tensor", "role"), split_axis=0, concat_axis=1, tiled=True)
    all_rows = devices * local_pre
    factor_count = 1
    while devices % (factor_count * 2) == 0 and factor_count * 2 * local_pre <= 512:
        factor_count = factor_count * 2
    block_rows = factor_count * local_pre
    blocks = received.reshape(all_rows // block_rows, block_rows, 2 * HEAD)

    def absorb(running, block_pair):
        row_max, row_total, summed = running
        block_number, shard_rows = block_pair
        row_start = block_number * block_rows
        key_seg = segment_of(row_start + jnp.arange(block_rows, dtype=jnp.int32), prefix_lens)
        visible = tok_seg[:, None] == key_seg[None, :]
        key_rows = shard_rows[:, :HEAD]
        value_rows = shard_rows[:, HEAD:]
        scores = jnp.where(
            visible,
            jnp.dot(queries, key_rows.T, preferred_element_type=jnp.float32) * score_scale,
            negative,
        )
        new_max = jnp.maximum(row_max, jnp.max(scores, axis=1))
        factor = jnp.exp(row_max - new_max)
        weights = jnp.where(visible, jnp.exp(scores - new_max[:, None]), 0.0)
        summed = summed * factor[:, None] + jnp.dot(
            weights.astype(jnp.bfloat16), value_rows, preferred_element_type=jnp.float32
        )
        return ((new_max, row_total * factor + jnp.sum(weights, axis=1), summed), None)

    numbers = jnp.arange(all_rows // block_rows, dtype=jnp.int32)
    (row_max, row_total, summed), unused = lax.scan(absorb, start_carry, (numbers, blocks))
    attention = (summed / row_total[:, None]).astype(jnp.bfloat16)
    stream_out = (
        floats
        + lax.psum_scatter(
            jnp.dot(attention, w_out, preferred_element_type=jnp.float32),
            ("tensor", "role"),
            scatter_dimension=0,
            tiled=True,
        )
    ).astype(jnp.bfloat16)
    owned = owner_dev == myself
    owned_count = jnp.sum(owned.astype(jnp.int32))
    starts = jnp.cumsum(span_lens) - span_lens
    first_row = jnp.sum(jnp.where(owned, starts, 0))
    length = jnp.sum(jnp.where(owned, span_lens, 0))
    target = jnp.sum(jnp.where(owned, offsets, 0))
    padded = jnp.concatenate(
        [keyval, jnp.zeros((span_rows, keyval.shape[1]), jnp.bfloat16)], axis=0
    )
    kv_block = lax.dynamic_slice_in_dim(padded, first_row, span_rows, 0)
    before = lax.dynamic_slice_in_dim(decode_cache, target, span_rows, 0)
    keep_new = (row_index < length) & (owned_count > 0)
    written = jnp.where(keep_new[:, None], kv_block, before)
    cache_out = lax.dynamic_update_slice_in_dim(decode_cache, written, target, 0)
    return (stream_out, cache_out)


def solution(mesh):
    in_specs = (
        P(("groups", "tensor", "role"), None),
        P(),
        P(None, ("tensor", "role")),
        P(None, ("tensor", "role")),
        P(("tensor", "role"), None),
        P(("groups", "tensor", "role"), None),
        P("groups"),
        P("groups"),
        P("groups"),
        P("groups"),
        P(("groups", "tensor", "role"), None),
    )
    out_specs = (P(("groups", "tensor", "role"), None), P(("groups", "tensor", "role"), None))
    return jax.shard_map(shards, mesh=mesh, in_specs=in_specs, out_specs=out_specs, check_vma=False)
```

profile of v0, /device:TPU:0, one launch (start us, length us, event | category | flops | bytes accessed | tf_op | source)
XLA Modules:
  0.0 209.1 jit_solution(15810380010315693694)
XLA Ops:
  7.2 1.2 copy.34
  8.4 0.7 convert_element_type.42
  9.1 1.1 fusion.13
  10.2 1.7 fusion.15
  11.9 1.0 reshape.80
  13.0 1.5 broadcast_in_dim.60
  14.5 7.6 %all-to-all-start = ((bf16[16,256,256]{2,1,0:T(8,128)(2,1)}), bf16[16,256,256]{2,1,0:T(8,128)(2,1)}, u32[]{:S(2)}, u32[]{:S(2)}) async-start(bf16[16,256,256]{2,1,0:T(8,128)(2,1)} %bitcast.30), calls=%async_computation | async-start | bytes 4194304 | tf_op jit(solution)/shard_map/all_to_all | solution.py:75
  22.6 56.1 %all-gather.2.cloned.1.call-done = bf16[128,8192]{1,0:T(8,128)(2,1)} async-done(((bf16[8,8192]{1,0:T(8,128)(2,1)}), bf16[128,8192]{1,0:T(8,128)(2,1)}) %all-gather.2.cloned.1.call-update) | async-done | bytes 2097168 | tf_op jit(solution)/shard_map/all_gather | solution.py:44
  78.7 2.5 %convolution_convert_fusion.1 = bf16[128,32]{0,1:T(8,128)(2,1)S(1)} fusion(bf16[128,8192]{1,0:T(8,128)(2,1)} %all-gather.2.cloned.1.call-done, bf16[8192,32]{0,1:T(8,128)(2,1)S(1)} %copy-done.4), kind=kOutput, calls=%fused_computation.22 | convolution fusion | flops 67112960 | bytes 2629632 | tf_op jit(solution)/shard_map/dot_general | solution.py:48
  81.3 17.7 %all_gather.7 = bf16[128,512]{0,1:T(8,128)(2,1)S(1)} all-gather(bf16[128,32]{0,1:T(8,128)(2,1)S(1)} %convolution_convert_fusion.1), channel_id=1, replica_groups=mesh['groups'=2,'tensor'=8,'role'=2] {'tensor','role'}, dimensions={1}, use_global_device_ids=true | all-gather | bytes 139264 | tf_op jit(solution)/shard_map/all_gather | solution.py:54
  99.0 2.3 %convolution_convert_fusion = bf16[128,128]{1,0:T(8,128)(2,1)S(1)} fusion(bf16[128,8192]{1,0:T(8,128)(2,1)S(1)} %copy-done.1, bf16[8192,128]{1,0:T(8,128)(2,1)} %param.15), kind=kOutput, calls=%fused_computation.21 | convolution fusion | flops 268451840 | bytes 4227072 | tf_op jit(solution)/shard_map/dot_general | solution.py:47
  101.6 0.3 fusion.21
  101.9 25.0 %while.16 = (s32[]{:T(128)}, f32[128]{0:T(128)S(1)}, f32[128]{0:T(128)S(1)}, f32[128,128]{1,0:T(8,128)S(1)}, s32[128]{0:T(128)S(1)}, /*index=5*/s32[8]{0:T(128)S...) while((s32[]{:T(128)}, f32[128]{0:T(128)S(1)}, ...), condition=%wide.region_10.11_spmd, body=%wide.region_6.10_spmd.sunk | while | flops 34386176 | bytes 1758893 | solution.py:105
  101.9 0.6 dynamic_slice.42
  103.2 1.0 dynamic-slice_bitcast_fusion.2
  104.2 0.2 fusion.51
  104.6 0.4 convolution_add_fusion.2
  105.0 0.6 dynamic_slice.42
  106.3 1.0 dynamic-slice_bitcast_fusion.2
  107.3 0.2 fusion.51
  107.7 0.4 convolution_add_fusion.2
  108.1 0.6 dynamic_slice.42
  109.5 1.0 dynamic-slice_bitcast_fusion.2
  110.4 0.2 fusion.51
  110.9 0.4 convolution_add_fusion.2
  111.3 0.6 dynamic_slice.42
  112.6 1.0 dynamic-slice_bitcast_fusion.2
  114.0 0.4 convolution_add_fusion.2
  114.4 0.6 dynamic_slice.42
  115.7 1.0 dynamic-slice_bitcast_fusion.2
  117.1 0.4 convolution_add_fusion.2
  117.5 0.6 dynamic_slice.42
  118.8 1.0 dynamic-slice_bitcast_fusion.2
  120.2 0.4 convolution_add_fusion.2
  120.6 0.6 dynamic_slice.42
  121.9 1.0 dynamic-slice_bitcast_fusion.2
  122.9 0.2 fusion.51
  123.3 0.4 convolution_add_fusion.2
  123.7 0.6 dynamic_slice.42
  125.1 1.0 dynamic-slice_bitcast_fusion.2
  126.5 0.4 convolution_add_fusion.2
  126.9 2.7 %fusion.23 = f32[128,8192]{1,0:T(8,128)} fusion(bf16[128,8192]{1,0:T(8,128)(2,1)S(1)} %copy-done, f32[128,128]{1,0:T(8,128)S(1)} %get-tuple-element.108, f32[128]{0:T(128)S(1)} %get-tuple-element.109), kind=kOutput, calls=%fused_computation.39 | convolution fusion | flops 268468224 | bytes 6357504 | tf_op jit(solution)/shard_map/dot_general | solution.py:110
  129.6 0.6 copy-done.6
  130.2 0.8 select_reduce_fusion.2
  135.5 0.7 compare_and_fusion
  136.4 1.2 dynamic_update_slice.3
  137.6 63.0 %reduce-scatter.2.cloned.1.call-done = f32[8,8192]{1,0:T(8,128)} async-done(((f32[128,8192]{1,0:T(8,128)}), f32[8,8192]{1,0:T(8,128)}) %reduce-scatter.2.cloned.1.call-update) | async-done | bytes 262160 | tf_op jit(solution)/shard_map/reduce_scatter | solution.py:109
  200.6 1.6 fusion.16
  (86 shorter events, 4.5 us)
Async XLA Ops:
  7.2 119.7 %copy-start = (bf16[128,8192]{1,0:T(8,128)(2,1)S(1)}, bf16[128,8192]{1,0:T(8,128)(2,1)}, u32[]{:S(2)}) copy-start(bf16[128,8192]{1,0:T(8,128)(2,1)} %param.17) | copy-start | bytes 6291460
  7.2 71.5 %all-gather.2.cloned.1.call-start = ((), (), s32[]{:S(2)}) async-start(), calls=%async_computation.2 | async-start | bytes 2228224 | tf_op jit(solution)/shard_map/all_gather | solution.py:44
  14.5 7.7 %copy-start.5 = (s32[8]{0:T(128)S(1)}, s32[8]{0:T(128)}, u32[]{:S(2)}) copy-start(s32[8]{0:T(128)} %param.19) | copy-start | bytes 100
  14.5 7.8 %copy-start.8 = (s32[8]{0:T(128)S(1)}, s32[8]{0:T(128)}, u32[]{:S(2)}) copy-start(s32[8]{0:T(128)} %param.20) | copy-start | bytes 100
  14.5 64.2 %copy-start.4 = (bf16[8192,32]{0,1:T(8,128)(2,1)S(1)}, bf16[8192,32]{0,1:T(8,128)(2,1)}, u32[]{:S(2)}) copy-start(bf16[8192,32]{0,1:T(8,128)(2,1)} %param.16) | copy-start | bytes 1572868
  14.5 87.4 %all-to-all-start = ((bf16[16,256,256]{2,1,0:T(8,128)(2,1)}), bf16[16,256,256]{2,1,0:T(8,128)(2,1)}, u32[]{:S(2)}, u32[]{:S(2)}) async-start(bf16[16,256,256]{2,1,0:T(8,128)(2,1)} %bitcast.30), calls=%async_computation | async-start | bytes 4194304 | tf_op jit(solution)/shard_map/all_to_all | solution.py:75
  22.1 178.6 %reduce-scatter.2.cloned.1.call-start = ((), (), s32[]{:S(2)}) async-start(), calls=%async_computation.3 | async-start | bytes 4456448 | tf_op jit(solution)/shard_map/reduce_scatter | solution.py:109
  78.7 20.2 %copy-start.1 = (bf16[128,8192]{1,0:T(8,128)(2,1)S(1)}, bf16[128,8192]{1,0:T(8,128)(2,1)}, u32[]{:S(2)}) copy-start(bf16[128,8192]{1,0:T(8,128)(2,1)} %all-gather.2.cloned.1.call-done) | copy-start | bytes 6291460
  129.5 0.7 copy-start.6
  129.5 0.7 copy-start.7
  129.5 71.1 %copy-start.2 = (bf16[8,8192]{1,0:T(8,128)(2,1)S(1)}, bf16[8,8192]{1,0:T(8,128)(2,1)}, u32[]{:S(2)}) copy-start(bf16[8,8192]{1,0:T(8,128)(2,1)} %param.13) | copy-start | bytes 393220
  137.6 64.6 %copy-start.3 = (bf16[512,512]{1,0:T(8,128)(2,1)}, bf16[512,512]{1,0:T(8,128)(2,1)S(1)}, u32[]{:S(2)}) copy-start(bf16[512,512]{1,0:T(8,128)(2,1)S(1)} %dynamic_update_slice.3) | copy-start | bytes 1572868
Sparse Core Ops, SparseCore 0:
  12.0 66.6 all-gather.1
  129.7 70.8 reduce-scatter.1
where the time goes:
time: 210 us; the launch traced here: 209 us
  waiting for transfers between devices  119 us (57%)
  between operations  18.6 us (9%)
  local copies, waits for them, and re-layouts  18.4 us (9%)
  blocking collectives  17.7 us (8%)
  matrix products  12.8 us (6%)
  other arithmetic  9.31 us (4%)
  starting transfers between devices  7.65 us (4%)
  loops' own time  5.54 us (3%)
    reduce_scatter x1, waiting for transfers between devices, shards(): lax.psum_scatter(jnp.dot(attention, w_out, preferred_element_type=jnp.flo...  63 us
    all_gather x1, waiting for transfers between devices, shards(): shard_rows = lax.all_gather(normed, ('tensor', 'role'), axis=0, tiled=True)  56.1 us
    all_gather x1, blocking collectives, shards(): keyval = lax.all_gather(kv_local, ('tensor', 'role'), axis=1, tiled=True)  17.7 us
    squeeze x8, local copies, waits for them, and re-layouts, shards(): lax.scan(absorb, start_carry, (numbers, blocks))  7.74 us
    all_to_all x1, starting transfers between devices, shards(): lax.all_to_all(repeated, ('tensor', 'role'), split_axis=0, concat_axis=1,...  7.57 us
    another operation x1, loops' own time, shards(): lax.scan(absorb, start_carry, (numbers, blocks))  5.54 us
    dynamic_slice x8, local copies, waits for them, and re-layouts, shards(): lax.scan(absorb, start_carry, (numbers, blocks))  4.69 us
  transfers between devices with their start and end apart: 3, of which 2 were waited for; matrix products, arithmetic and copies ran while one was open for 5% of the time, Pallas kernels for 0%

commit v1 on v0

--- a/solution.py
+++ b/solution.py
@@ -1,6 +1,8 @@
 import jax
 import jax.numpy as jnp
 from jax import lax
+from jax.experimental import pallas as pl
+from jax.experimental.pallas import tpu as pltpu
 from jax.sharding import PartitionSpec as P
 
 HEAD = 128
@@ -130,6 +132,447 @@
     return (stream_out, cache_out)
 
 
+MESH = pl.DeviceIdType.MESH
+F32 = jnp.float32
+BF16 = jnp.bfloat16
+CW, CCW = 0, 1
+
+
+def chip_at(position, chips):
+    back = position // (chips // 2)
+    return (1 - back) * 2 * position + back * (2 * (chips - 1 - position) + 1)
+
+
+def fused(
+    x_ref,
+    gain_ref,
+    span_ref,
+    plen_ref,
+    owner_ref,
+    offset_ref,
+    wq_hbm,
+    wkv_hbm,
+    wout_hbm,
+    pre_hbm,
+    dec_hbm,
+    out_ref,
+    cache_ref,
+    wq,
+    wkv,
+    wout,
+    dec,
+    normed,
+    xsend,
+    xrecv,
+    kvbuf,
+    kvt,
+    scores,
+    part,
+    peer_out,
+    peer_in,
+    ring_out,
+    ring_in,
+    lsem,
+    xs,
+    xr,
+    ags,
+    agr,
+    pfs,
+    pfr,
+    p1s,
+    p1r,
+    p2s,
+    p2r,
+    pps,
+    ppr,
+    kvs,
+    kvr,
+    pes,
+    per,
+    rss,
+    rsr,
+):
+    chips = lax.axis_size("tensor")
+    devices = 2 * chips
+    t = lax.axis_index("tensor")
+    c = lax.axis_index("role")
+    peer = 1 - c
+    d = 2 * t + c
+    odd = t % 2
+    pos = (1 - odd) * (t // 2) + odd * (chips - 1 - t // 2)
+    nxt = chip_at((pos + 1) % chips, chips)
+    prv = chip_at((pos + chips - 1) % chips, chips)
+    width = x_ref.shape[1]
+    half = width // 2
+    quarter = width // 4
+    tokens = 16 * chips
+    pre_rows = pre_hbm.shape[0]
+    all_pre = devices * pre_rows
+    g = t // 4
+    u = t % 4
+
+    def remote(src, dst, ssem, rsem, tt, cc):
+        return pltpu.make_async_remote_copy(
+            src_ref=src,
+            dst_ref=dst,
+            send_sem=ssem,
+            recv_sem=rsem,
+            device_id={"tensor": tt, "role": cc},
+            device_id_type=MESH,
+        )
+
+    sent = []
+
+    def send(*args):
+        copy = remote(*args)
+        copy.start()
+        sent.append(copy)
+
+    barrier = pltpu.get_barrier_semaphore()
+    for r in range(1, devices):
+        other = (d + r) % devices
+        pl.semaphore_signal(
+            barrier, inc=1, device_id={"tensor": other // 2, "role": other % 2}, device_id_type=MESH
+        )
+
+    def pre_slot(index):
+        return kvbuf.at[pl.ds(pl.multiple_of(index * pre_rows, pre_rows), pre_rows), :]
+
+    def head_columns(head):
+        return pre_hbm.at[:, pl.ds(pl.multiple_of(head * 2 * HEAD, 2 * HEAD), 2 * HEAD)]
+
+    loads = [
+        pltpu.make_async_copy(head_columns(g), pre_slot(d), lsem.at[0]),
+        pltpu.make_async_copy(wkv_hbm, wkv, lsem.at[1]),
+        pltpu.make_async_copy(wq_hbm, wq, lsem.at[2]),
+        pltpu.make_async_copy(wout_hbm, wout, lsem.at[3]),
+        pltpu.make_async_copy(dec_hbm, dec, lsem.at[4]),
+    ]
+    for load in loads:
+        load.start()
+
+    floats = x_ref[...].astype(F32)
+    mine = floats * lax.rsqrt(jnp.mean(floats * floats, axis=1, keepdims=True) + epsilon)
+    mine = mine * gain_ref[...].astype(F32)
+    is_one = (c == 1).astype(F32)
+    left, right = mine[:, :half], mine[:, half:]
+    xsend[...] = jnp.where(is_one > 0.5, left, right).astype(BF16)
+    kept = jnp.where(is_one > 0.5, right, left).astype(BF16).astype(F32)
+
+    pl.semaphore_wait(barrier, devices - 1)
+    send(xsend, xrecv, xs, xr, t, peer)
+
+    def block(chip, core, h=None):
+        column = core * half if h is None else core * half + h * quarter
+        size = half if h is None else quarter
+        return (
+            pl.ds(pl.multiple_of(16 * chip, 16), 16),
+            pl.ds(pl.multiple_of(column, quarter), size),
+        )
+
+    remote(xsend, xrecv, xs, xr, t, peer).wait_recv()
+    theirs = xrecv[...].astype(F32)
+    first = jnp.where(is_one > 0.5, theirs, kept)
+    second = jnp.where(is_one > 0.5, kept, theirs)
+    normed[block(t, c)] = jnp.concatenate([first, second], axis=0).astype(BF16)
+
+    def source(way, hops):
+        return chip_at((pos + chips - hops) % chips if way == CW else (pos + hops) % chips, chips)
+
+    def hop(way, s, h):
+        here = normed.at[block(source(way, s), c, h)]
+        send(here, here, ags.at[way, s, h], agr.at[way, s, h], (nxt, prv)[way], c)
+
+    last = chips // 2 - 1
+    own = normed.at[block(t, c)]
+    messages = [(s, h, way) for s in range(last + 1) for h in range(2) for way in (CW, CCW)]
+    messages = [m for m in messages if m[0] < last or m[1] == m[2]]
+    for s, h, way in messages:
+        if s == 0:
+            hop(way, 0, h)
+    send(own, own, pfs.at[0, last, 1], pfr.at[0, last, 1], t, peer)
+    for s, h, way in messages:
+        landed = normed.at[block(source(way, s + 1), c, h)]
+        remote(landed, landed, ags.at[way, s, h], agr.at[way, s, h], nxt, c).wait_recv()
+        if (s + 1, h, way) in messages:
+            hop(way, s + 1, h)
+        send(landed, landed, pfs.at[way, s, h], pfr.at[way, s, h], t, peer)
+        if (s, h, way) == messages[1]:
+            other_half = (t + 4) % chips
+            send(
+                head_columns(1 - g), pre_slot(d), p1s, p1r, other_half, c
+            )
+
+    loads[0].wait()
+    partner = 2 * ((t + 4) % chips) + c
+
+    def spread(index, which):
+        for j in range(1, 4):
+            send(pre_slot(index), pre_slot(index), p2s.at[j, which], p2r.at[j, which], 4 * g + (u + j) % 4, c)
+        send(pre_slot(index), pre_slot(index), pps.at[0, which], ppr.at[0, which], t, peer)
+
+    spread(d, 0)
+    remote(pre_slot(partner), pre_slot(partner), p1s, p1r, t, peer).wait_recv()
+    spread(partner, 1)
+
+    own = normed.at[block(t, peer)]
+    remote(own, own, pfs.at[0, last, 1], pfr.at[0, last, 1], t, peer).wait_recv()
+    for s, h, way in messages:
+        landed = normed.at[block(source(way, s + 1), peer, h)]
+        remote(landed, landed, pfs.at[way, s, h], pfr.at[way, s, h], t, peer).wait_recv()
+    loads[1].wait()
+    kv = jnp.dot(normed[...], wkv[...], preferred_element_type=F32)
+    kv_rows = wkv.shape[1]
+
+    def kv_slot(index):
+        return kvt.at[pl.ds(pl.multiple_of(index * kv_rows, kv_rows), kv_rows), :]
+
+    kv_slot(d)[...] = jnp.transpose(kv).astype(BF16)
+    for r in range(1, devices):
+        other = (d + r) % devices
+        send(kv_slot(d), kv_slot(d), kvs.at[r], kvr.at[r], other // 2, other % 2)
+    loads[2].wait()
+    queries = jnp.dot(normed[...], wq[...], preferred_element_type=F32).astype(BF16)
+
+    def segments(positions, ref):
+        end = 0
+        total = jnp.zeros_like(positions)
+        for r in range(ref.shape[0]):
+            end = end + ref[r]
+            total = total + (positions >= end).astype(jnp.int32)
+        return total
+
+    tok_col = segments(lax.broadcasted_iota(jnp.int32, (tokens, 1), 0), span_ref)
+    tok_row = segments(lax.broadcasted_iota(jnp.int32, (1, tokens), 1), span_ref)
+
+    for which in range(2):
+        for j in range(1, 4):
+            chip = 4 * g + (u + 4 - j) % 4
+            chip = chip if which == 0 else (chip + 4) % chips
+            slot = pre_slot(2 * chip + c)
+            remote(slot, slot, p2s.at[j, which], p2r.at[j, which], t, peer).wait_recv()
+            send(slot, slot, pps.at[j, which], ppr.at[j, which], t, peer)
+    for r in range(1, devices):
+        slot = kv_slot((d + devices - r) % devices)
+        remote(slot, slot, kvs.at[r], kvr.at[r], t, peer).wait_recv()
+    score_scale = 1.0 / HEAD**0.5
+    key_base = pl.multiple_of(g * 2 * HEAD, 2 * HEAD)
+    span_keys = kvt[pl.ds(key_base, HEAD), :]
+    span_values = kvt[pl.ds(key_base + HEAD, HEAD), :]
+    before = lax.broadcasted_iota(jnp.int32, (tokens, tokens), 0) >= lax.broadcasted_iota(
+        jnp.int32, (tokens, tokens), 1
+    )
+    span_mask = (tok_col == tok_row) & before
+    span_scores = jnp.where(
+        span_mask, jnp.dot(queries, span_keys, preferred_element_type=F32) * score_scale, negative
+    )
+    for which in range(2):
+        for j in range(4):
+            chip = 4 * g + (u + 4 - j) % 4
+            chip = chip if which == 0 else (chip + 4) % chips
+            slot = pre_slot(2 * chip + peer)
+            remote(slot, slot, pps.at[j, which], ppr.at[j, which], t, peer).wait_recv()
+
+    tile = 512
+    nt = (((1,), (1,)), ((), ()))
+    seen = []
+    row_max = jnp.max(span_scores, axis=1, keepdims=True)
+    for i in range(all_pre // tile):
+        place = lax.broadcasted_iota(jnp.int32, (1, tile), 1) + i * tile
+        seg = segments(place, plen_ref)
+        seen.append(seg)
+        raw = lax.dot_general(
+            queries, kvbuf[i * tile : (i + 1) * tile, :HEAD], nt, preferred_element_type=F32
+        )
+        masked = jnp.where(tok_col == seg, raw * score_scale, negative)
+        scores[:, i * tile : (i + 1) * tile] = masked
+        row_max = jnp.maximum(row_max, jnp.max(masked, axis=1, keepdims=True))
+    weights = jnp.where(span_mask, jnp.exp(span_scores - row_max), 0.0)
+    row_total = jnp.sum(weights, axis=1, keepdims=True)
+    summed = lax.dot_general(weights.astype(BF16), span_values, nt, preferred_element_type=F32)
+    for i in range(all_pre // tile):
+        weights = jnp.exp(scores[:, i * tile : (i + 1) * tile] - row_max)
+        weights = jnp.where(tok_col == seen[i], weights, 0.0)
+        row_total = row_total + jnp.sum(weights, axis=1, keepdims=True)
+        summed = summed + jnp.dot(
+            weights.astype(BF16),
+            kvbuf[i * tile : (i + 1) * tile, HEAD:],
+            preferred_element_type=F32,
+        )
+    attention = (summed / row_total).astype(BF16)
+
+    loads[3].wait()
+    step = 1024
+    for i in range(width // step):
+        part[:, i * step : (i + 1) * step] = jnp.dot(
+            attention, wout[:, i * step : (i + 1) * step], preferred_element_type=F32
+        )
+
+    def stacked(k, core, h):
+        rows = pl.ds(pl.multiple_of(16 * chip_at((pos + k) % chips, chips) + 8 * core, 8), 8)
+        top = part[rows, h * quarter : (h + 1) * quarter]
+        bottom = part[rows, half + h * quarter : half + (h + 1) * quarter]
+        return jnp.concatenate([top, bottom], axis=0)
+
+    order = [4, 3, 5, 2, 6, 1, 7, 0]
+    for k in order:
+        for h in range(2):
+            peer_out[k, :, h * quarter : (h + 1) * quarter] = stacked(k, peer, h).astype(BF16)
+        send(peer_out.at[k], peer_in.at[k], pes.at[k], per.at[k], t, peer)
+
+    def summand(k, h):
+        return stacked(k, c, h) + peer_in[k, :, h * quarter : (h + 1) * quarter].astype(F32)
+
+    def from_peer(k):
+        remote(peer_out.at[k], peer_in.at[k], pes.at[k], per.at[k], t, peer).wait_recv()
+
+    def from_ring(way, s, h):
+        remote(
+            ring_out.at[way, s, h], ring_in.at[way, s, h], rss.at[way, s, h], rsr.at[way, s, h], nxt, c
+        ).wait_recv()
+        return ring_in[way, s, h].astype(F32)
+
+    hops = [(s, h, way) for s in range(4) for h in range(2) for way in (CW, CCW)]
+    hops = [m for m in hops if m[0] > 0 or m[1] == m[2]]
+    ready = []
+    for s, h, way in hops:
+        k = 4 - s if way == CW else 4 + s
+        if k not in ready:
+            from_peer(k)
+            ready.append(k)
+        value = summand(k, h)
+        if (s - 1, h, way) in hops:
+            value = value + from_ring(way, s - 1, h)
+        ring_out[way, s, h] = value.astype(BF16)
+        send(
+            ring_out.at[way, s, h],
+            ring_in.at[way, s, h],
+            rss.at[way, s, h],
+            rsr.at[way, s, h],
+            (nxt, prv)[way],
+            c,
+        )
+
+    first_row = 0
+    length = 0
+    target = 0
+    start = 0
+    for r in range(span_ref.shape[0]):
+        own_it = (owner_ref[r] == d).astype(jnp.int32)
+        first_row = first_row + own_it * start
+        length = length + own_it * span_ref[r]
+        target = target + own_it * offset_ref[r]
+        start = start + span_ref[r]
+    loads[4].wait()
+    cache_rows = dec.shape[0]
+    row = lax.broadcasted_iota(jnp.int32, (cache_rows, tokens), 0) - target
+    token = lax.broadcasted_iota(jnp.int32, (cache_rows, tokens), 1)
+    picks = ((token - first_row) == row) & (row >= 0) & (row < length)
+    picked = lax.dot_general(
+        picks.astype(F32).astype(BF16), kvt[...], nt, preferred_element_type=F32
+    )
+    row = lax.broadcasted_iota(jnp.int32, (cache_rows, 1), 0) - target
+    written = jnp.where((row >= 0) & (row < length), picked, dec[...].astype(F32))
+    cache_ref[...] = written.astype(BF16)
+
+    from_peer(0)
+    for h in range(2):
+        value = summand(0, h) + from_ring(CW, 3, h) + from_ring(CCW, 3, h)
+        for side in range(2):
+            columns = slice(side * half + h * quarter, side * half + (h + 1) * quarter)
+            out_ref[:, columns] = (
+                x_ref[:, columns].astype(F32) + value[8 * side : 8 * side + 8]
+            ).astype(BF16)
+    for copy in sent:
+        copy.wait_send()
+
+
+def fused_shards(
+    stream_in,
+    norm_gain,
+    w_query,
+    w_keyval,
+    w_out,
+    prefix_cache,
+    span_lens,
+    prefix_lens,
+    owner_dev,
+    offsets,
+    decode_cache,
+):
+    chips = lax.axis_size("tensor")
+    devices = 2 * chips
+    rows, width = stream_in.shape
+    tokens = rows * devices
+    pre_rows = prefix_cache.shape[0]
+    quarter = width // 4
+    vmem = pl.BlockSpec(memory_space=pltpu.VMEM)
+    smem = pl.BlockSpec(memory_space=pltpu.SMEM)
+    hbm = pl.BlockSpec(memory_space=pl.ANY)
+    dma = pltpu.SemaphoreType.DMA
+    return pl.pallas_call(
+        fused,
+        out_shape=(
+            jax.ShapeDtypeStruct(stream_in.shape, BF16),
+            jax.ShapeDtypeStruct(decode_cache.shape, BF16),
+        ),
+        in_specs=[vmem, vmem] + [smem] * 4 + [hbm] * 5,
+        out_specs=(vmem, vmem),
+        scratch_shapes=[
+            pltpu.VMEM(w_query.shape, BF16),
+            pltpu.VMEM(w_keyval.shape, BF16),
+            pltpu.VMEM(w_out.shape, BF16),
+            pltpu.VMEM(decode_cache.shape, BF16),
+            pltpu.VMEM((tokens, width), BF16),
+            pltpu.VMEM((8, width // 2), BF16),
+            pltpu.VMEM((8, width // 2), BF16),
+            pltpu.VMEM((devices * pre_rows, 2 * HEAD), BF16),
+            pltpu.VMEM((devices * w_keyval.shape[1], tokens), BF16),
+            pltpu.VMEM((tokens, devices * pre_rows), F32),
+            pltpu.VMEM((tokens, width), F32),
+            pltpu.VMEM((chips, 16, width // 2), BF16),
+            pltpu.VMEM((chips, 16, width // 2), BF16),
+            pltpu.VMEM((2, 4, 2, 16, quarter), BF16),
+            pltpu.VMEM((2, 4, 2, 16, quarter), BF16),
+            dma((5,)),
+            dma,
+            dma,
+            dma((2, 4, 2)),
+            dma((2, 4, 2)),
+            dma((2, 4, 2)),
+            dma((2, 4, 2)),
+            dma,
+            dma,
+            dma((4, 2)),
+            dma((4, 2)),
+            dma((4, 2)),
+            dma((4, 2)),
+            dma((devices,)),
+            dma((devices,)),
+            dma((chips,)),
+            dma((chips,)),
+            dma((2, 4, 2)),
+            dma((2, 4, 2)),
+        ],
+        compiler_params=pltpu.CompilerParams(
+            collective_id=0, has_side_effects=True, vmem_limit_bytes=48 * 1024 * 1024
+        ),
+        name="fused_attention",
+    )(
+        stream_in,
+        norm_gain.reshape(1, width),
+        span_lens,
+        prefix_lens,
+        owner_dev,
+        offsets,
+        w_query,
+        w_keyval,
+        w_out,
+        prefix_cache,
+        decode_cache,
+    )
+
+
 def solution(mesh):
     in_specs = (
         P(("groups", "tensor", "role"), None),
@@ -145,4 +588,6 @@
         P(("groups", "tensor", "role"), None),
     )
     out_specs = (P(("groups", "tensor", "role"), None), P(("groups", "tensor", "role"), None))
-    return jax.shard_map(shards, mesh=mesh, in_specs=in_specs, out_specs=out_specs, check_vma=False)
+    small = mesh.shape["tensor"] == 8 and mesh.shape["role"] == 2
+    body = fused_shards if small else shards
+    return jax.shard_map(body, mesh=mesh, in_specs=in_specs, out_specs=out_specs, check_vma=False)

time: 210 us -> 69.6 us (0.33)
  waiting for transfers between devices: 119 us -> 0 us
  Pallas kernels: 0 us -> 62.8 us
  between operations: 18.6 us -> 0.77 us
  blocking collectives: 17.7 us -> 0 us
  matrix products: 12.8 us -> 0 us
  local copies, waits for them, and re-layouts: 18.4 us -> 5.81 us
  other arithmetic: 9.31 us -> 0 us
  starting transfers between devices: 7.65 us -> 0 us
  loops' own time: 5.54 us -> 0 us
    reduce_scatter x1 -> x0, waiting for transfers between devices: 63 us -> none  [shards(): lax.psum_scatter(jnp.dot(attention, w_out, preferred_element_type=jnp.flo...]
    pallas_call x0 -> x1, Pallas kernels: none -> 62.8 us  [fused_shards(): pl.pallas_call(fused, out_shape=(jax.ShapeDtypeStruct(stream_in.shape, BF...]
    all_gather x1 -> x0, waiting for transfers between devices: 56.1 us -> none  [shards(): shard_rows = lax.all_gather(normed, ('tensor', 'role'), axis=0, tiled=True)]
    all_gather x1 -> x0, blocking collectives: 17.7 us -> none  [shards(): keyval = lax.all_gather(kv_local, ('tensor', 'role'), axis=1, tiled=True)]
    dot_general x21 -> x0, matrix products: 12.8 us -> none  [the longest x8 2.93 us: absorb(): jnp.dot(weights.astype(jnp.bfloat16), value_rows, preferred_element_type=...]
    squeeze x8 -> x0, local copies, waits for them, and re-layouts: 7.74 us -> none  [shards(): lax.scan(absorb, start_carry, (numbers, blocks))]
    all_to_all x1 -> x0, starting transfers between devices: 7.57 us -> none  [shards(): lax.all_to_all(repeated, ('tensor', 'role'), split_axis=0, concat_axis=1,...]
    another operation x1 -> x0, loops' own time: 5.54 us -> none  [shards(): lax.scan(absorb, start_carry, (numbers, blocks))]
  transfers between devices with their start and end apart: 3 -> 0, of which waited for: 2 -> 0; matrix products, arithmetic and copies ran while one was open for 5% -> 0% of each run, Pallas kernels for 0% -> 0%
where the time goes in v1:
time: 69.6 us; the launch traced here: 69.4 us
  Pallas kernels  62.8 us (90%)
  local copies, waits for them, and re-layouts  5.81 us (8%)
  between operations  0.77 us (1%)
    pallas_call x1, Pallas kernels, fused_shards(): pl.pallas_call(fused, out_shape=(jax.ShapeDtypeStruct(stream_in.shape, BF...  62.8 us
    unnamed x19, local copies, waits for them, and re-layouts  5 us

profile of v1, /device:TPU:0, one launch (start us, length us, event | category | flops | bytes accessed | tf_op | source)
XLA Modules:
  0.0 69.4 jit_solution(5059375578286040104)
XLA Ops:
  0.6 0.0 copy-start.1
  0.6 0.0 copy-start.7
  0.7 0.0 copy-start.6
  0.7 0.0 copy-start.5
  0.7 0.0 copy-start.4
  0.7 0.0 copy-start.2
  0.7 0.0 copy-start.3
  0.7 0.8 %reshape.7.gain_ref = bf16[1,8192]{1,0:T(2,128)(2,1)S(1)} reshape(bf16[8192]{0:T(1024)(128)(2,1)} %param.12) | data formatting | bytes 32768 | tf_op jit(solution)/shard_map/reshape | solution.py:563
  1.5 1.9 %copy.13.wkv_hbm = bf16[8192,32]{1,0:T(8,128)(2,1)S(1)} copy(bf16[8192,32]{0,1:T(8,128)(2,1)} %param.14) | data formatting | bytes 1048576 | tf_op args[3]
  3.5 0.0 copy-done.1
  3.5 0.0 copy-done.7
  3.5 0.0 copy-done.6
  3.5 0.0 copy-done.5
  3.5 0.0 copy-done.4
  3.5 0.0 copy-done.2
  3.5 0.0 copy-done.3
  3.5 0.0 copy-start
  3.5 1.6 %copy-done = bf16[8192,128]{1,0:T(8,128)(2,1)S(1)} copy-done((bf16[8192,128]{1,0:T(8,128)(2,1)S(1)}, bf16[8192,128]{1,0:T(8,128)(2,1)}, u32[]{:S(2)}) %copy-start) | copy-done | bytes 2097176
  5.1 62.8 %fused_attention.1 = (bf16[8,8192]{1,0:T(8,128)(2,1)S(1)}, bf16[512,512]{1,0:T(8,128)(2,1)S(1)}) custom-call(bf16[8,8192]{1,0:T(8,128)(2,1)S(1)} %copy-done.3, bf16[1,8192]{1,0:T(2,128)(2,1)S(1)} %reshape.7.gain_ref, s32[8]{0:T(128)S(1)} %copy-done.4, s32[8]{0:T(128)S(1)} %copy-done.5, s32[8]{0:T(128)S(1)} %copy-done.6, s32[8]{0:T(128)S(1)} %copy-done.7, ...), custom_call_target="tpu_custom_call" | custom-call | tf_op jit(solution)/shard_map/fused_attention/pallas_call | solution.py:513
  67.9 0.7 copy.16
  68.6 0.8 %copy.17 = bf16[512,512]{1,0:T(8,128)(2,1)} copy(bf16[512,512]{1,0:T(8,128)(2,1)S(1)} %get-tuple-element.5) | data formatting | bytes 1048576
Async XLA Ops:
  0.6 2.8 %copy-start.1 = (bf16[512,512]{1,0:T(8,128)(2,1)S(1)}, bf16[512,512]{1,0:T(8,128)(2,1)}, u32[]{:S(2)}) copy-start(bf16[512,512]{1,0:T(8,128)(2,1)} %dec_hbm.1) | copy-start | bytes 1572868
  0.6 2.8 %copy-start.7 = (s32[8]{0:T(128)S(1)}, s32[8]{0:T(128)}, u32[]{:S(2)}) copy-start(s32[8]{0:T(128)} %offset_ref.1) | copy-start | bytes 100
  0.7 2.8 %copy-start.6 = (s32[8]{0:T(128)S(1)}, s32[8]{0:T(128)}, u32[]{:S(2)}) copy-start(s32[8]{0:T(128)} %owner_ref.1) | copy-start | bytes 100
  0.7 2.8 %copy-start.5 = (s32[8]{0:T(128)S(1)}, s32[8]{0:T(128)}, u32[]{:S(2)}) copy-start(s32[8]{0:T(128)} %plen_ref.1) | copy-start | bytes 100
  0.7 2.8 %copy-start.4 = (s32[8]{0:T(128)S(1)}, s32[8]{0:T(128)}, u32[]{:S(2)}) copy-start(s32[8]{0:T(128)} %span_ref.1) | copy-start | bytes 100
  0.7 2.8 %copy-start.2 = (bf16[256,512]{1,0:T(8,128)(2,1)S(1)}, bf16[256,512]{1,0:T(8,128)(2,1)}, u32[]{:S(2)}) copy-start(bf16[256,512]{1,0:T(8,128)(2,1)} %pre_hbm.1) | copy-start | bytes 786436
  0.7 2.8 %copy-start.3 = (bf16[8,8192]{1,0:T(8,128)(2,1)S(1)}, bf16[8,8192]{1,0:T(8,128)(2,1)}, u32[]{:S(2)}) copy-start(bf16[8,8192]{1,0:T(8,128)(2,1)} %x_ref.1) | copy-start | bytes 393220
  3.5 1.6 %copy-start = (bf16[8192,128]{1,0:T(8,128)(2,1)S(1)}, bf16[8192,128]{1,0:T(8,128)(2,1)}, u32[]{:S(2)}) copy-start(bf16[8192,128]{1,0:T(8,128)(2,1)} %wq_hbm.1) | copy-start | bytes 6291460

commit v2 on v1

--- a/solution.py
+++ b/solution.py
@@ -166,6 +166,9 @@
     xrecv,
     kvbuf,
     kvt,
+    qall,
+    sums_out,
+    sums_in,
     scores,
     part,
     peer_out,
@@ -187,6 +190,10 @@
     ppr,
     kvs,
     kvr,
+    qs,
+    qr,
+    ss,
+    sr,
     pes,
     per,
     rss,
@@ -207,9 +214,10 @@
     quarter = width // 4
     tokens = 16 * chips
     pre_rows = pre_hbm.shape[0]
-    all_pre = devices * pre_rows
     g = t // 4
-    u = t % 4
+    y = t % 2
+    across = t + 1 - 2 * y
+    along = t + 2 - 4 * ((t // 2) % 2)
 
     def remote(src, dst, ssem, rsem, tt, cc):
         return pltpu.make_async_remote_copy(
@@ -235,14 +243,15 @@
             barrier, inc=1, device_id={"tensor": other // 2, "role": other % 2}, device_id_type=MESH
         )
 
-    def pre_slot(index):
+    def pre_slot(which, row, core):
+        index = which * 4 + row * 2 + core
         return kvbuf.at[pl.ds(pl.multiple_of(index * pre_rows, pre_rows), pre_rows), :]
 
     def head_columns(head):
         return pre_hbm.at[:, pl.ds(pl.multiple_of(head * 2 * HEAD, 2 * HEAD), 2 * HEAD)]
 
     loads = [
-        pltpu.make_async_copy(head_columns(g), pre_slot(d), lsem.at[0]),
+        pltpu.make_async_copy(head_columns(g), pre_slot(0, y, c), lsem.at[0]),
         pltpu.make_async_copy(wkv_hbm, wkv, lsem.at[1]),
         pltpu.make_async_copy(wq_hbm, wq, lsem.at[2]),
         pltpu.make_async_copy(wout_hbm, wout, lsem.at[3]),
@@ -253,7 +262,7 @@
 
     floats = x_ref[...].astype(F32)
     mine = floats * lax.rsqrt(jnp.mean(floats * floats, axis=1, keepdims=True) + epsilon)
-    mine = mine * gain_ref[...].astype(F32)
+    mine = mine * gain_ref[...].astype(F32).reshape(1, width)
     is_one = (c == 1).astype(F32)
     left, right = mine[:, :half], mine[:, half:]
     xsend[...] = jnp.where(is_one > 0.5, left, right).astype(BF16)
@@ -297,23 +306,16 @@
         if (s + 1, h, way) in messages:
             hop(way, s + 1, h)
         send(landed, landed, pfs.at[way, s, h], pfr.at[way, s, h], t, peer)
-        if (s, h, way) == messages[1]:
-            other_half = (t + 4) % chips
-            send(
-                head_columns(1 - g), pre_slot(d), p1s, p1r, other_half, c
-            )
 
     loads[0].wait()
-    partner = 2 * ((t + 4) % chips) + c
-
-    def spread(index, which):
-        for j in range(1, 4):
-            send(pre_slot(index), pre_slot(index), p2s.at[j, which], p2r.at[j, which], 4 * g + (u + j) % 4, c)
-        send(pre_slot(index), pre_slot(index), pps.at[0, which], ppr.at[0, which], t, peer)
-
-    spread(d, 0)
-    remote(pre_slot(partner), pre_slot(partner), p1s, p1r, t, peer).wait_recv()
-    spread(partner, 1)
+    send(head_columns(1 - g), pre_slot(1, y, c), p1s, p1r, (t + 4) % chips, c)
+
+    def spread(which):
+        slot = pre_slot(which, y, c)
+        send(slot, slot, p2s.at[which], p2r.at[which], across, c)
+        send(slot, slot, pps.at[which, 0], ppr.at[which, 0], t, peer)
+
+    spread(0)
 
     own = normed.at[block(t, peer)]
     remote(own, own, pfs.at[0, last, 1], pfr.at[0, last, 1], t, peer).wait_recv()
@@ -321,18 +323,24 @@
         landed = normed.at[block(source(way, s + 1), peer, h)]
         remote(landed, landed, pfs.at[way, s, h], pfr.at[way, s, h], t, peer).wait_recv()
     loads[1].wait()
-    kv = jnp.dot(normed[...], wkv[...], preferred_element_type=F32)
-    kv_rows = wkv.shape[1]
+    nt = (((1,), (1,)), ((), ()))
+    kv = lax.dot_general(wkv[...], normed[...], nt, preferred_element_type=F32)
+    kv_rows = wkv.shape[0]
 
     def kv_slot(index):
         return kvt.at[pl.ds(pl.multiple_of(index * kv_rows, kv_rows), kv_rows), :]
 
-    kv_slot(d)[...] = jnp.transpose(kv).astype(BF16)
+    kv_slot(d)[...] = kv.astype(BF16)
     for r in range(1, devices):
         other = (d + r) % devices
         send(kv_slot(d), kv_slot(d), kvs.at[r], kvr.at[r], other // 2, other % 2)
     loads[2].wait()
     queries = jnp.dot(normed[...], wq[...], preferred_element_type=F32).astype(BF16)
+    qall[:tokens, :] = queries
+    send(qall.at[pl.ds(0, tokens)], qall.at[pl.ds(tokens, tokens)], qs, qr, along, c)
+    slot = pre_slot(1, y, c)
+    remote(slot, slot, p1s, p1r, t, peer).wait_recv()
+    spread(1)
 
     def segments(positions, ref):
         end = 0
@@ -345,17 +353,68 @@
     tok_col = segments(lax.broadcasted_iota(jnp.int32, (tokens, 1), 0), span_ref)
     tok_row = segments(lax.broadcasted_iota(jnp.int32, (1, tokens), 1), span_ref)
 
-    for which in range(2):
-        for j in range(1, 4):
-            chip = 4 * g + (u + 4 - j) % 4
-            chip = chip if which == 0 else (chip + 4) % chips
-            slot = pre_slot(2 * chip + c)
-            remote(slot, slot, p2s.at[j, which], p2r.at[j, which], t, peer).wait_recv()
-            send(slot, slot, pps.at[j, which], ppr.at[j, which], t, peer)
+    def wait_slot(slot, ssem, rsem):
+        remote(slot, slot, ssem, rsem, t, peer).wait_recv()
+
+    score_scale = 1.0 / HEAD**0.5
+    tok_two = jnp.concatenate([tok_col, tok_col], axis=0)
+    tile = 2 * pre_rows
+    seen = []
+    tops = None
+    wait_slot(pre_slot(0, 1 - y, c), p2s.at[0], p2r.at[0])
+    send(pre_slot(0, 1 - y, c), pre_slot(0, 1 - y, c), pps.at[0, 1], ppr.at[0, 1], t, peer)
+    remote(
+        qall.at[pl.ds(0, tokens)], qall.at[pl.ds(tokens, tokens)], qs, qr, t, peer
+    ).wait_recv()
+    pieces = [(0, 0), (0, 1), (1, 0), (1, 1)]
+
+    def piece_rows(which, rel):
+        chip_row = y if rel == 0 else 1 - y
+        return pl.ds(pl.multiple_of((which * 2 + chip_row) * tile, tile), tile)
+
+    for i, (which, rel) in enumerate(pieces):
+        chip_row = y if rel == 0 else 1 - y
+        if (which, rel) == (1, 1):
+            wait_slot(pre_slot(1, chip_row, c), p2s.at[1], p2r.at[1])
+            slot = pre_slot(1, chip_row, c)
+            send(slot, slot, pps.at[1, 1], ppr.at[1, 1], t, peer)
+        wait_slot(pre_slot(which, chip_row, peer), pps.at[which, rel], ppr.at[which, rel])
+        chip = (2 * (t // 2) + 4 * which) % chips + chip_row
+        seg = segments(lax.broadcasted_iota(jnp.int32, (1, tile), 1) + chip * tile, plen_ref)
+        seen.append(seg)
+        raw = lax.dot_general(
+            qall[...], kvbuf[piece_rows(which, rel), :HEAD], nt, preferred_element_type=F32
+        )
+        masked = jnp.where(tok_two == seg, raw * score_scale, negative)
+        scores[:, i * tile : (i + 1) * tile] = masked
+        top = jnp.max(masked, axis=1, keepdims=True)
+        tops = top if tops is None else jnp.maximum(tops, top)
+
+    def absorb(first_row):
+        rows = slice(first_row, first_row + tokens)
+        top = tops[rows]
+        total = jnp.zeros((tokens, 1), F32)
+        product = jnp.zeros((tokens, HEAD), F32)
+        for i, (which, rel) in enumerate(pieces):
+            weights = jnp.exp(scores[rows, i * tile : (i + 1) * tile] - top)
+            weights = jnp.where(tok_col == seen[i], weights, 0.0)
+            total = total + jnp.sum(weights, axis=1, keepdims=True)
+            product = product + jnp.dot(
+                weights.astype(BF16), kvbuf[piece_rows(which, rel), HEAD:], preferred_element_type=F32
+            )
+        return top, total, product
+
+    top, total, product = absorb(tokens)
+    lane = lax.broadcasted_iota(jnp.int32, (tokens, tokens), 1)
+    turned = jnp.transpose(jnp.where(lane < tokens // 2, top, total))
+    sums_out[:tokens, :] = product
+    sums_out[tokens:, :] = turned[tokens // 2 - 8 : tokens // 2 + 8]
+    send(sums_out, sums_in, ss, sr, along, c)
+    top, total, product = absorb(0)
+
     for r in range(1, devices):
         slot = kv_slot((d + devices - r) % devices)
         remote(slot, slot, kvs.at[r], kvr.at[r], t, peer).wait_recv()
-    score_scale = 1.0 / HEAD**0.5
     key_base = pl.multiple_of(g * 2 * HEAD, 2 * HEAD)
     span_keys = kvt[pl.ds(key_base, HEAD), :]
     span_values = kvt[pl.ds(key_base + HEAD, HEAD), :]
@@ -366,39 +425,18 @@
     span_scores = jnp.where(
         span_mask, jnp.dot(queries, span_keys, preferred_element_type=F32) * score_scale, negative
     )
-    for which in range(2):
-        for j in range(4):
-            chip = 4 * g + (u + 4 - j) % 4
-            chip = chip if which == 0 else (chip + 4) % chips
-            slot = pre_slot(2 * chip + peer)
-            remote(slot, slot, pps.at[j, which], ppr.at[j, which], t, peer).wait_recv()
-
-    tile = 512
-    nt = (((1,), (1,)), ((), ()))
-    seen = []
-    row_max = jnp.max(span_scores, axis=1, keepdims=True)
-    for i in range(all_pre // tile):
-        place = lax.broadcasted_iota(jnp.int32, (1, tile), 1) + i * tile
-        seg = segments(place, plen_ref)
-        seen.append(seg)
-        raw = lax.dot_general(
-            queries, kvbuf[i * tile : (i + 1) * tile, :HEAD], nt, preferred_element_type=F32
-        )
-        masked = jnp.where(tok_col == seg, raw * score_scale, negative)
-        scores[:, i * tile : (i + 1) * tile] = masked
-        row_max = jnp.maximum(row_max, jnp.max(masked, axis=1, keepdims=True))
+    remote(sums_out, sums_in, ss, sr, t, peer).wait_recv()
+    turned = jnp.transpose(jnp.concatenate([sums_in[tokens:, :]] * (tokens // 16), axis=0))
+    other_top, other_total = turned[:, 0:1], turned[:, 8:9]
+    span_top = jnp.max(span_scores, axis=1, keepdims=True)
+    row_max = jnp.maximum(jnp.maximum(top, other_top), span_top)
     weights = jnp.where(span_mask, jnp.exp(span_scores - row_max), 0.0)
-    row_total = jnp.sum(weights, axis=1, keepdims=True)
+    factor, other_factor = jnp.exp(top - row_max), jnp.exp(other_top - row_max)
+    row_total = (
+        jnp.sum(weights, axis=1, keepdims=True) + total * factor + other_total * other_factor
+    )
     summed = lax.dot_general(weights.astype(BF16), span_values, nt, preferred_element_type=F32)
-    for i in range(all_pre // tile):
-        weights = jnp.exp(scores[:, i * tile : (i + 1) * tile] - row_max)
-        weights = jnp.where(tok_col == seen[i], weights, 0.0)
-        row_total = row_total + jnp.sum(weights, axis=1, keepdims=True)
-        summed = summed + jnp.dot(
-            weights.astype(BF16),
-            kvbuf[i * tile : (i + 1) * tile, HEAD:],
-            preferred_element_type=F32,
-        )
+    summed = summed + product * factor + sums_in[:tokens, :] * other_factor
     attention = (summed / row_total).astype(BF16)
 
     loads[3].wait()
@@ -520,15 +558,18 @@
         out_specs=(vmem, vmem),
         scratch_shapes=[
             pltpu.VMEM(w_query.shape, BF16),
-            pltpu.VMEM(w_keyval.shape, BF16),
+            pltpu.VMEM((w_keyval.shape[1], width), BF16),
             pltpu.VMEM(w_out.shape, BF16),
             pltpu.VMEM(decode_cache.shape, BF16),
             pltpu.VMEM((tokens, width), BF16),
             pltpu.VMEM((8, width // 2), BF16),
             pltpu.VMEM((8, width // 2), BF16),
-            pltpu.VMEM((devices * pre_rows, 2 * HEAD), BF16),
+            pltpu.VMEM((devices // 2 * pre_rows, 2 * HEAD), BF16),
             pltpu.VMEM((devices * w_keyval.shape[1], tokens), BF16),
-            pltpu.VMEM((tokens, devices * pre_rows), F32),
+            pltpu.VMEM((2 * tokens, HEAD), BF16),
+            pltpu.VMEM((tokens + 16, HEAD), F32),
+            pltpu.VMEM((tokens + 16, HEAD), F32),
+            pltpu.VMEM((2 * tokens, devices // 2 * pre_rows), F32),
             pltpu.VMEM((tokens, width), F32),
             pltpu.VMEM((chips, 16, width // 2), BF16),
             pltpu.VMEM((chips, 16, width // 2), BF16),
@@ -543,30 +584,34 @@
             dma((2, 4, 2)),
             dma,
             dma,
-            dma((4, 2)),
-            dma((4, 2)),
-            dma((4, 2)),
-            dma((4, 2)),
+            dma((2,)),
+            dma((2,)),
+            dma((2, 2)),
+            dma((2, 2)),
             dma((devices,)),
             dma((devices,)),
+            dma,
+            dma,
+            dma,
+            dma,
             dma((chips,)),
             dma((chips,)),
             dma((2, 4, 2)),
             dma((2, 4, 2)),
         ],
         compiler_params=pltpu.CompilerParams(
-            collective_id=0, has_side_effects=True, vmem_limit_bytes=48 * 1024 * 1024
+            collective_id=0, has_side_effects=True, vmem_limit_bytes=60 * 1024 * 1024
         ),
         name="fused_attention",
     )(
         stream_in,
-        norm_gain.reshape(1, width),
+        norm_gain,
         span_lens,
         prefix_lens,
         owner_dev,
         offsets,
         w_query,
-        w_keyval,
+        w_keyval.T,
         w_out,
         prefix_cache,
         decode_cache,

time: 69.6 us -> 65.8 us (0.945)
  local copies, waits for them, and re-layouts: 5.81 us -> 3.44 us
  Pallas kernels: 62.8 us -> 61.5 us
    unnamed x19 -> x2, local copies, waits for them, and re-layouts: 5 us -> 3.44 us
    pallas_call x1, Pallas kernels: 62.8 us -> 61.5 us  [fused_shards(): pl.pallas_call(fused, out_shape=(jax.ShapeDtypeStruct(stream_in.shape, BF...]
    reshape x1 -> x0, local copies, waits for them, and re-layouts: 0.81 us -> none  [fused_shards(): norm_gain.reshape(1, width)]
where the time goes in v2:
time: 65.8 us; the launch traced here: 65.6 us
  Pallas kernels  61.5 us (93%)
  local copies, waits for them, and re-layouts  3.44 us (5%)
    pallas_call x1, Pallas kernels, fused_shards(): pl.pallas_call(fused, out_shape=(jax.ShapeDtypeStruct(stream_in.shape, BF...  61.5 us
    unnamed x2, local copies, waits for them, and re-layouts  3.44 us

profile of v2, /device:TPU:0, one launch (start us, length us, event | category | flops | bytes accessed | tf_op | source)
XLA Modules:
  0.0 65.6 jit_solution(6433255459317031946)
XLA Ops:
  0.6 61.5 %fused_attention.1 = (bf16[8,8192]{1,0:T(8,128)(2,1)}, bf16[512,512]{1,0:T(8,128)(2,1)}) custom-call(bf16[8,8192]{1,0:T(8,128)(2,1)} %x_ref.1, bf16[8192]{0:T(1024)(128)(2,1)} %gain_ref.1, s32[8]{0:T(128)} %span_ref.1, s32[8]{0:T(128)} %plen_ref.1, s32[8]{0:T(128)} %owner_ref.1, s32[8]{0:T(128)} %offset_ref.1, bf16[8192,128]{1,0:T(8,128)(2,1)} %wq_hbm.1, ...), custom_call_target="tpu_custom_call" | custom-call | tf_op jit(solution)/shard_map/fused_attention/pallas_call | solution.py:551
  62.2 1.6 %copy.15 = bf16[8,8192]{1,0:T(8,128)(2,1)} copy(bf16[8,8192]{1,0:T(8,128)(2,1)} %get-tuple-element.4) | data formatting | bytes 262144
  63.7 1.9 %copy.16 = bf16[512,512]{1,0:T(8,128)(2,1)} copy(bf16[512,512]{1,0:T(8,128)(2,1)} %get-tuple-element.5) | data formatting | bytes 1048576

commit v3 on v2

--- a/solution.py
+++ b/solution.py
@@ -296,6 +296,7 @@
     own = normed.at[block(t, c)]
     messages = [(s, h, way) for s in range(last + 1) for h in range(2) for way in (CW, CCW)]
     messages = [m for m in messages if m[0] < last or m[1] == m[2]]
+    messages = sorted(messages, key=lambda m: (m[0], m[1] != m[2]))
     for s, h, way in messages:
         if s == 0:
             hop(way, 0, h)
@@ -306,9 +307,10 @@
         if (s + 1, h, way) in messages:
             hop(way, s + 1, h)
         send(landed, landed, pfs.at[way, s, h], pfr.at[way, s, h], t, peer)
+        if (s, h, way) == (last - 1, 0, CCW):
+            send(head_columns(1 - g), pre_slot(1, y, c), p1s, p1r, (t + 4) % chips, c)
 
     loads[0].wait()
-    send(head_columns(1 - g), pre_slot(1, y, c), p1s, p1r, (t + 4) % chips, c)
 
     def spread(which):
         slot = pre_slot(which, y, c)
@@ -472,6 +474,9 @@
 
     hops = [(s, h, way) for s in range(4) for h in range(2) for way in (CW, CCW)]
     hops = [m for m in hops if m[0] > 0 or m[1] == m[2]]
+    hops = [m for m in hops if m[0] == 0] + sorted(
+        [m for m in hops if m[0] > 0], key=lambda m: (m[0], m[1] == m[2])
+    )
     ready = []
     for s, h, way in hops:
         k = 4 - s if way == CW else 4 + s

time: 65.8 us -> 61.9 us (0.941)
  Pallas kernels: 61.5 us -> 57.7 us
    pallas_call x1, Pallas kernels: 61.5 us -> 57.7 us  [fused_shards(): pl.pallas_call(fused, out_shape=(jax.ShapeDtypeStruct(stream_in.shape, BF...]
where the time goes in v3:
time: 61.9 us; the launch traced here: 61.8 us
  Pallas kernels  57.7 us (93%)
  local copies, waits for them, and re-layouts  3.44 us (6%)
  between operations  0.64 us (1%)
    pallas_call x1, Pallas kernels, fused_shards(): pl.pallas_call(fused, out_shape=(jax.ShapeDtypeStruct(stream_in.shape, BF...  57.7 us
    unnamed x2, local copies, waits for them, and re-layouts  3.44 us

profile of v3, /device:TPU:0, one launch (start us, length us, event | category | flops | bytes accessed | tf_op | source)
XLA Modules:
  0.0 61.8 jit_solution(14376656924166530568)
XLA Ops:
  0.6 57.7 %fused_attention.1 = (bf16[8,8192]{1,0:T(8,128)(2,1)}, bf16[512,512]{1,0:T(8,128)(2,1)}) custom-call(bf16[8,8192]{1,0:T(8,128)(2,1)} %x_ref.1, bf16[8192]{0:T(1024)(128)(2,1)} %gain_ref.1, s32[8]{0:T(128)} %span_ref.1, s32[8]{0:T(128)} %plen_ref.1, s32[8]{0:T(128)} %owner_ref.1, s32[8]{0:T(128)} %offset_ref.1, bf16[8192,128]{1,0:T(8,128)(2,1)} %wq_hbm.1, ...), custom_call_target="tpu_custom_call" | custom-call | tf_op jit(solution)/shard_map/fused_attention/pallas_call | solution.py:556
  58.3 1.6 %copy.15 = bf16[8,8192]{1,0:T(8,128)(2,1)} copy(bf16[8,8192]{1,0:T(8,128)(2,1)} %get-tuple-element.4) | data formatting | bytes 262144
  59.9 1.9 %copy.16 = bf16[512,512]{1,0:T(8,128)(2,1)} copy(bf16[512,512]{1,0:T(8,128)(2,1)} %get-tuple-element.5) | data formatting | bytes 1048576

commit v4 on v3

--- a/solution.py
+++ b/solution.py
@@ -530,6 +530,22 @@
         copy.wait_send()
 
 
+def hand_over(stream_ref, cache_ref, stream_out, cache_out, stream_held, cache_held, sems):
+    pairs = [
+        (stream_ref, stream_held, stream_out),
+        (cache_ref, cache_held, cache_out),
+    ]
+    into = [pltpu.make_async_copy(a, b, sems.at[i]) for i, (a, b, _) in enumerate(pairs)]
+    out = [pltpu.make_async_copy(b, e, sems.at[2 + i]) for i, (_, b, e) in enumerate(pairs)]
+    for copy in into:
+        copy.start()
+    for arrival, departure in zip(into, out):
+        arrival.wait()
+        departure.start()
+    for copy in out:
+        copy.wait()
+
+
 def fused_shards(
     stream_in,
     norm_gain,
@@ -553,7 +569,7 @@
     smem = pl.BlockSpec(memory_space=pltpu.SMEM)
     hbm = pl.BlockSpec(memory_space=pl.ANY)
     dma = pltpu.SemaphoreType.DMA
-    return pl.pallas_call(
+    results = pl.pallas_call(
         fused,
         out_shape=(
             jax.ShapeDtypeStruct(stream_in.shape, BF16),
@@ -621,6 +637,21 @@
         prefix_cache,
         decode_cache,
     )
+    return pl.pallas_call(
+        hand_over,
+        out_shape=(
+            jax.ShapeDtypeStruct(stream_in.shape, BF16),
+            jax.ShapeDtypeStruct(decode_cache.shape, BF16),
+        ),
+        in_specs=[hbm, hbm],
+        out_specs=(hbm, hbm),
+        scratch_shapes=[
+            pltpu.VMEM(stream_in.shape, BF16),
+            pltpu.VMEM(decode_cache.shape, BF16),
+            dma((4,)),
+        ],
+        name="hand_over",
+    )(*results)
 
 
 def solution(mesh):

time: 61.9 us -> 60.4 us (0.976)
  local copies, waits for them, and re-layouts: 3.44 us -> 0 us
  Pallas kernels: 57.7 us -> 59.6 us
    unnamed x2 -> x0, local copies, waits for them, and re-layouts: 3.44 us -> none
    pallas_call x0 -> x1, Pallas kernels: none -> 1.94 us  [fused_shards(): pl.pallas_call(hand_over, out_shape=(jax.ShapeDtypeStruct(stream_in.shape...]
where the time goes in v4:
time: 60.4 us; the launch traced here: 60.3 us
  Pallas kernels  59.6 us (99%)
  between operations  0.64 us (1%)
    pallas_call x1, Pallas kernels, fused_shards(): pl.pallas_call(fused, out_shape=(jax.ShapeDtypeStruct(stream_in.shape, BF...  57.7 us
    pallas_call x1, Pallas kernels, fused_shards(): pl.pallas_call(hand_over, out_shape=(jax.ShapeDtypeStruct(stream_in.shape...  1.94 us

profile of v4, /device:TPU:0, one launch (start us, length us, event | category | flops | bytes accessed | tf_op | source)
XLA Modules:
  0.0 60.3 jit_solution(6816987173759421286)
XLA Ops:
  0.6 57.7 %fused_attention.1 = (bf16[8,8192]{1,0:T(8,128)(2,1)}, bf16[512,512]{1,0:T(8,128)(2,1)}) custom-call(bf16[8,8192]{1,0:T(8,128)(2,1)} %x_ref.1, bf16[8192]{0:T(1024)(128)(2,1)} %gain_ref.1, s32[8]{0:T(128)} %span_ref.1, s32[8]{0:T(128)} %plen_ref.1, s32[8]{0:T(128)} %owner_ref.1, s32[8]{0:T(128)} %offset_ref.1, bf16[8192,128]{1,0:T(8,128)(2,1)} %wq_hbm.1, ...), custom_call_target="tpu_custom_call" | custom-call | tf_op jit(solution)/shard_map/fused_attention/pallas_call | solution.py:572
  58.3 1.9 %hand_over.1 = (bf16[8,8192]{1,0:T(8,128)(2,1)}, bf16[512,512]{1,0:T(8,128)(2,1)}) custom-call(bf16[8,8192]{1,0:T(8,128)(2,1)} %get-tuple-element.4.stream_ref, bf16[512,512]{1,0:T(8,128)(2,1)} %get-tuple-element.5.cache_ref), custom_call_target="tpu_custom_call" | custom-call | tf_op jit(solution)/shard_map/hand_over/pallas_call | solution.py:640

commit v5 on v4

--- a/solution.py
+++ b/solution.py
@@ -301,6 +301,13 @@
         if s == 0:
             hop(way, 0, h)
     send(own, own, pfs.at[0, last, 1], pfr.at[0, last, 1], t, peer)
+    loads[0].wait()
+
+    def spread(which):
+        slot = pre_slot(which, y, c)
+        send(slot, slot, p2s.at[which], p2r.at[which], across, c)
+        send(slot, slot, pps.at[which, 0], ppr.at[which, 0], t, peer)
+
     for s, h, way in messages:
         landed = normed.at[block(source(way, s + 1), c, h)]
         remote(landed, landed, ags.at[way, s, h], agr.at[way, s, h], nxt, c).wait_recv()
@@ -309,15 +316,7 @@
         send(landed, landed, pfs.at[way, s, h], pfr.at[way, s, h], t, peer)
         if (s, h, way) == (last - 1, 0, CCW):
             send(head_columns(1 - g), pre_slot(1, y, c), p1s, p1r, (t + 4) % chips, c)
-
-    loads[0].wait()
-
-    def spread(which):
-        slot = pre_slot(which, y, c)
-        send(slot, slot, p2s.at[which], p2r.at[which], across, c)
-        send(slot, slot, pps.at[which, 0], ppr.at[which, 0], t, peer)
-
-    spread(0)
+            spread(0)
 
     own = normed.at[block(t, peer)]
     remote(own, own, pfs.at[0, last, 1], pfr.at[0, last, 1], t, peer).wait_recv()

time: 60.4 us -> 60.4 us (level)
  no operation moved by 1% of the time
where the time goes in v5:
time: 60.4 us; the launch traced here: 60.2 us
  Pallas kernels  59.6 us (99%)
  between operations  0.64 us (1%)
    pallas_call x1, Pallas kernels, fused_shards(): pl.pallas_call(fused, out_shape=(jax.ShapeDtypeStruct(stream_in.shape, BF...  57.6 us
    pallas_call x1, Pallas kernels, fused_shards(): pl.pallas_call(hand_over, out_shape=(jax.ShapeDtypeStruct(stream_in.shape...  1.94 us

profile of v5, /device:TPU:0, one launch (start us, length us, event | category | flops | bytes accessed | tf_op | source)
XLA Modules:
  0.0 60.2 jit_solution(4726794095714233086)
XLA Ops:
  0.6 57.6 %fused_attention.1 = (bf16[8,8192]{1,0:T(8,128)(2,1)}, bf16[512,512]{1,0:T(8,128)(2,1)}) custom-call(bf16[8,8192]{1,0:T(8,128)(2,1)} %x_ref.1, bf16[8192]{0:T(1024)(128)(2,1)} %gain_ref.1, s32[8]{0:T(128)} %span_ref.1, s32[8]{0:T(128)} %plen_ref.1, s32[8]{0:T(128)} %owner_ref.1, s32[8]{0:T(128)} %offset_ref.1, bf16[8192,128]{1,0:T(8,128)(2,1)} %wq_hbm.1, ...), custom_call_target="tpu_custom_call" | custom-call | tf_op jit(solution)/shard_map/fused_attention/pallas_call | solution.py:571
  58.3 1.9 %hand_over.1 = (bf16[8,8192]{1,0:T(8,128)(2,1)}, bf16[512,512]{1,0:T(8,128)(2,1)}) custom-call(bf16[8,8192]{1,0:T(8,128)(2,1)} %get-tuple-element.4.stream_ref, bf16[512,512]{1,0:T(8,128)(2,1)} %get-tuple-element.5.cache_ref), custom_call_target="tpu_custom_call" | custom-call | tf_op jit(solution)/shard_map/hand_over/pallas_call | solution.py:639
